TPU v7x, 128 devices: a whole 4x4x4 slice. The times are simulated.
128 devices in a mesh: section: 8 (over x_hi, y), dp: 16 (over z, x_lo, core).
Axes of the slice: x: 4 (x_hi: 2, x_lo: 2; x = x_hi * 2 + x_lo), y: 4, z: 4, core: 2. Of those that a mesh axis runs over, the one named last changes fastest.
Arguments:
- acts_in: bfloat16 [2, 128, 6144], P(None, 'dp'), may hold values from -6 to 6
- weights: bfloat16 [8, 6144, 6144], P('section', None, 'dp'), may hold values from -0.078125 to 0.078125
- gains: float32 [8, 6144], P('section'), may hold values from 0.25 to 1.75
- stored: bfloat16 [8, 64, 8, 6144], P('section', 'dp'), may hold values from -6 to 6
- sample_ids: int32 [2, 16], P(None, 'dp'), may hold values from 0 to 63, as said below
- cotangent: bfloat16 [2, 128, 6144], P(None, 'dp'), may hold values from -0.1796875 to 0.1796875
Outputs:
- new_stored: bfloat16 [8, 64, 8, 6144], P('section', 'dp')
- grad_weight: float32 [8, 6144, 6144], P('section', None, 'dp')
- grad_gain: float32 [8, 6144], P('section')
Inputs may be any that keep to these rules, and one draw needn't show every extreme that they name: `sample_ids`: column k names slots k * 4 to (k + 1) * 4 - 1 only, and the 2 micro-batches name different slots in each column.
All inputs are finite; a program needn't handle non-finite values.
Results may differ from a plain program's by a relative error of at most 0.04.
Values may be sent and summed in bfloat16 or wider, within the bound.
A program may use at most 704 MiB of HBM per device.

v0:
```python
import functools

import jax
import jax.numpy as jnp
from jax import lax
from jax.experimental import pallas as pl
from jax.experimental.pallas import tpu as pltpu
from jax.sharding import PartitionSpec as P

MESH = pl.DeviceIdType.MESH
F32 = jnp.float32
BF16 = jnp.bfloat16

clip_limit = 1.0
epsilon = 1e-05
gelu_coeff = 0.7978845608028654


def gelu_value(values):
    inner = gelu_coeff * (values + 0.044715 * values * values * values)
    return 0.5 * values * (1.0 + jnp.tanh(inner))


def gelu_slope(values):
    tangent = jnp.tanh(gelu_coeff * (values + 0.044715 * values * values * values))
    return 0.5 * (1.0 + tangent) + 0.5 * values * (1.0 - tangent * tangent) * gelu_coeff * (
        1.0 + 0.134145 * values * values
    )


def relay(
    sections,
    groups,
    ids,
    acts_hbm,
    weights,
    gains_hbm,
    stored_hbm,
    cotangent_hbm,
    arrived_out,
    normed_out,
    slope_out,
    gain_out,
    acts,
    gains,
    stored,
    cotangent,
    wbuf,
    nbuf,
    gbuf,
    xbuf,
    pout,
    pin,
    hidden,
    incoming,
    arrived,
    arr_in,
    slopes,
    slope_in,
    ybuf,
    back_out,
    back_in,
    up_in,
    up_out,
    scales,
    xturned,
    partial_sum,
    gain_sum,
    gain_row,
    gain_in,
    gain_full,
    load_sem,
    w_sem,
    gather_send,
    gather_recv,
    part_send,
    part_recv,
    slope_send,
    slope_recv,
    back_send,
    back_recv,
    side_send,
    side_recv,
    keep_send,
    keep_recv,
    copy_sem,
    gain_sem,
):
    micro, seg_rows, width = acts.shape
    half = width // 2
    own_cols = weights.shape[2]
    chip_cols = 2 * own_cols
    chips = groups // 2
    rows = chips * seg_rows
    slot_count = stored.shape[1]
    section = lax.axis_index("section")
    me = lax.axis_index("dp")
    core = lax.rem(me, 2)
    chip = lax.div(me, 2)
    sibling = me + 1 - 2 * core
    first = section == 0
    last = section == sections - 1
    after = lax.rem(section + 1, sections)
    before = lax.rem(section + sections - 1, sections)
    step_k = 1024
    parts = 3
    span = half // parts
    z_count = groups // 4
    z_pos = lax.div(me, 4)
    x_pos = lax.rem(chip, 2)

    loads = [
        pltpu.make_async_copy(source, target, load_sem.at[i])
        for i, (source, target) in enumerate(
            (
                (acts_hbm, acts),
                (stored_hbm, stored),
                (gains_hbm, gains),
                (cotangent_hbm, cotangent),
            )
        )
    ]
    for load in loads:
        load.start()
    own_place = pl.ds(pl.multiple_of(core * own_cols, 128), own_cols)
    weight_own = pltpu.make_async_copy(
        weights.at[0, pl.ds(core * half, half), :], wbuf.at[:, own_place], w_sem.at[2]
    )
    weight_own.start()

    barrier = pltpu.get_barrier_semaphore()

    def greet(step, carry):
        other = lax.rem(me + step, groups)
        for there in (after, before):
            pl.semaphore_signal(
                barrier, inc=1, device_id={"section": there, "dp": other}, device_id_type=MESH
            )

        @pl.when(step > 0)
        def _():
            pl.semaphore_signal(
                barrier, inc=1, device_id={"section": section, "dp": other}, device_id_type=MESH
            )

        return carry

    lax.fori_loop(0, groups, greet, 0)
    pl.semaphore_wait(barrier, 3 * groups - 1)

    weight_share = pltpu.make_async_remote_copy(
        src_ref=weights.at[0, pl.ds((1 - core) * half, half), :],
        dst_ref=wbuf.at[:, own_place],
        send_sem=w_sem.at[0],
        recv_sem=w_sem.at[1],
        device_id={"dp": sibling},
        device_id_type=MESH,
    )
    weight_share.start()
    loads[0].wait()
    loads[1].wait()
    loads[2].wait()
    loads[3].wait()
    gain_sum[...] = jnp.zeros_like(gain_sum)

    def remote(source, target, send, recv, there, other):
        return pltpu.make_async_remote_copy(
            src_ref=source,
            dst_ref=target,
            send_sem=send,
            recv_sem=recv,
            device_id={"section": there, "dp": other},
            device_id_type=MESH,
        )

    def far_z(i):
        away = jnp.where(i == 3, 0, jnp.where(i == 0, 2, 2 * i - 1))
        return lax.rem(z_pos + away, z_count)

    def far_device(i):
        x = lax.rem(x_pos + 1 - lax.rem(lax.div(i, 2), 2), 2)
        return far_z(lax.div(i, 4)) * 4 + x * 2 + lax.rem(core + 1 - lax.rem(i, 2), 2)

    def far_chip(i):
        return far_z(lax.div(i, 2)) * 2 + lax.rem(x_pos + 1 - lax.rem(i, 2), 2)

    def await_bytes(ref, sem):
        pltpu.make_async_copy(ref, ref, sem).wait()

    def keep_place(m, chain):
        return pl.ds(pl.multiple_of((m * 2 + chain) * rows, rows), rows)

    def turned_place(m):
        wide = 2 * rows
        return (
            pl.ds(pl.multiple_of(core * half, half), half),
            pl.ds(pl.multiple_of(m * wide, wide), wide),
        )

    def keep_share(m):
        return remote(
            xturned.at[m],
            normed_out.at[turned_place(m)],
            keep_send.at[m],
            keep_recv.at[m],
            section,
            sibling,
        )

    def keep_own(m):
        return pltpu.make_async_copy(
            xturned.at[m], normed_out.at[turned_place(m)], copy_sem.at[0, m, 0]
        )

    def turn_normed(m):
        for k in range(0, half, step_k):
            piece = xbuf[m, :, :, k : k + step_k].reshape(2 * rows, step_k).astype(F32)
            xturned[m, k : k + step_k, :] = jnp.transpose(piece).astype(BF16)
        keep_share(m).start()
        keep_own(m).start()

    def slope_copy(m, chain):
        return pltpu.make_async_copy(
            ybuf.at[m, chain, :, own_place],
            slope_out.at[keep_place(m, chain), :],
            copy_sem.at[1, m, chain],
        )

    def send_slopes(kind, m, there, remote_own):
        def send(step, carry):
            other = far_device(step)
            remote(
                slopes.at[kind, m, lax.div(other, 2)],
                slope_in.at[m, core, chip],
                slope_send.at[kind, m],
                slope_recv.at[m, core],
                there,
                other,
            ).start()
            return carry

        if remote_own:
            lax.fori_loop(0, groups, send, 0)
        else:
            lax.fori_loop(0, groups - 1, send, 0)
            pltpu.make_async_copy(
                slopes.at[kind, m, chip], slope_in.at[m, core, chip], slope_recv.at[m, core]
            ).start()

    def part(q):
        return slice(q * chip_cols, (q + 1) * chip_cols)

    def summed_parts(kind, m, q):
        return pin[kind, m, 2 * q].astype(F32) + pin[kind, m, 2 * q + 1].astype(F32)

    def forward_rows(m):
        @pl.when(first)
        def _():
            incoming[...] = acts[m].astype(F32)

        @pl.when(jnp.logical_not(first))
        def _():
            await_bytes(arr_in.at[m], side_recv.at[0, m])
            await_bytes(pin.at[0, m], part_recv.at[0, m])
            for q in range(chips):
                value = summed_parts(0, m, q)
                hidden[m, :, part(q)] = value
                total = arr_in[m, :, part(q)].astype(F32) + gelu_value(value)
                incoming[:, part(q)] = total.astype(BF16).astype(F32)

        slot = jnp.clip(ids[m, 0] - me * slot_count, 0, slot_count - 1)
        previous = stored[0, slot].astype(F32)
        moved = jnp.clip(incoming[...] - previous, -clip_limit, clip_limit)
        arrived_now = (previous + moved).astype(BF16)
        arrived[m] = arrived_now
        arrived_f = arrived_now.astype(F32)
        scale = lax.rsqrt(jnp.mean(arrived_f * arrived_f, axis=-1, keepdims=True) + epsilon)
        scales[m] = jnp.broadcast_to(scale, (seg_rows, 128))
        normed = (arrived_f * scale * gains[...]).astype(BF16)
        for side in range(2):
            for p in range(parts):
                start = side * half + p * span
                nbuf[m, p, side] = normed[:, start : start + span]
        for p in range(parts):

            def send(step, carry, p=p):
                other = far_device(step)
                remote(
                    nbuf.at[m, p, lax.rem(other, 2)],
                    gbuf.at[m, core, p, chip],
                    gather_send.at[m],
                    gather_recv.at[m, core, p],
                    section,
                    other,
                ).start()
                return carry

            lax.fori_loop(0, groups - 1, send, 0)
            pltpu.make_async_copy(
                nbuf.at[m, p, core], gbuf.at[m, core, p, chip], gather_recv.at[m, core, p]
            ).start()

        @pl.when(jnp.logical_not(last))
        def _():
            remote(
                arrived.at[m], arr_in.at[m], side_send.at[0, m], side_recv.at[0, m], after, me
            ).start()

        @pl.when(jnp.logical_not(first))
        def _():
            for q in range(chips):
                hidden[m, :, part(q)] = gelu_slope(hidden[m, :, part(q)])

    def forward_columns(m, chain):
        @pl.when((m == 0) & (chain == 0))
        def _():
            weight_own.wait()
            weight_share.wait_recv()

        for p in range(parts):
            await_bytes(gbuf.at[m, chain, p], gather_recv.at[m, chain, p])
            base = p * span
            for k in range(0, span, step_k):
                piece = gbuf[m, chain, p, :, :, k : k + step_k].astype(F32).reshape(rows, step_k)
                xbuf[m, chain, :, base + k : base + k + step_k] = piece.astype(BF16)
            for c in range(0, chip_cols, 256):
                product = jnp.dot(
                    xbuf[m, chain, :, base : base + span],
                    wbuf[base : base + span, c : c + 256],
                    preferred_element_type=F32,
                )
                if p > 0:
                    product = product + partial_sum[:, c : c + 256]
                if p + 1 < parts:
                    partial_sum[:, c : c + 256] = product
                else:
                    shaped = product.reshape(chips, seg_rows, 256).astype(BF16)
                    pout[m, chain, :, :, c : c + 256] = shaped

        def send(step, carry):
            q = far_chip(step)
            other = 2 * q + chain

            @pl.when(jnp.logical_not(last))
            def _():
                remote(
                    pout.at[m, chain, q],
                    pin.at[0, m, me],
                    part_send.at[m, chain],
                    part_recv.at[0, m],
                    after,
                    other,
                ).start()

            @pl.when(last & (other != me))
            def _():
                remote(
                    pout.at[m, chain, q],
                    pin.at[1, m, me],
                    part_send.at[m, chain],
                    part_recv.at[1, m],
                    section,
                    other,
                ).start()

            return carry

        lax.fori_loop(0, chips, send, 0)

        @pl.when(last & (core == chain))
        def _():
            pltpu.make_async_copy(
                pout.at[m, chain, chip], pin.at[1, m, me], part_recv.at[1, m]
            ).start()

    def turn_rows(m):
        await_bytes(pin.at[1, m], part_recv.at[1, m])
        for q in range(chips):
            slope = cotangent[m, :, part(q)].astype(F32) * gelu_slope(summed_parts(1, m, q))
            slopes[1, m, q] = slope.astype(BF16)
        send_slopes(1, m, section, False)

    def backward_columns(m, chain):
        await_bytes(slope_in.at[m, chain], slope_recv.at[m, chain])
        ybuf[m, chain] = slope_in[m, chain].astype(F32).reshape(rows, chip_cols).astype(BF16)
        for p in range(parts):
            for k in range(0, span, step_k):
                product = lax.dot_general(
                    ybuf[m, chain],
                    wbuf[p * span + k : p * span + k + step_k, :],
                    (((1,), (1,)), ((), ())),
                    preferred_element_type=F32,
                )
                shaped = product.reshape(chips, seg_rows, step_k).astype(BF16)
                back_out[m, chain, p, :, :, k : k + step_k] = shaped

            def send(step, carry, p=p):
                q = far_chip(step)
                other = 2 * q + chain

                @pl.when(other != me)
                def _():
                    remote(
                        back_out.at[m, chain, p, q],
                        back_in.at[m, p, me],
                        back_send.at[m, chain],
                        back_recv.at[m],
                        section,
                        other,
                    ).start()

                return carry

            @pl.when(jnp.logical_not(first))
            def _(p=p, send=send):
                lax.fori_loop(0, chips, send, 0)

            @pl.when(jnp.logical_not(first) & (core == chain))
            def _(p=p):
                pltpu.make_async_copy(
                    back_out.at[m, chain, p, chip], back_in.at[m, p, me], back_recv.at[m]
                ).start()

        for p in range(parts):
            for k in range(0, span, step_k):
                term = back_out[m, chain, p, :, :, k : k + step_k].astype(F32) * gbuf[
                    m, chain, p, :, :, k : k + step_k
                ].astype(F32)
                place = slice(p * span + k, p * span + k + step_k)
                gain_sum[:, place] += jnp.sum(term, axis=0)
        slope_copy(m, chain).start()

    def backward_rows(m):
        @pl.when(last)
        def _():
            up_in[m] = cotangent[m]

        @pl.when(jnp.logical_not(last))
        def _():
            await_bytes(up_in.at[m], side_recv.at[1, m])

        await_bytes(back_in.at[m], back_recv.at[m])
        pieces = []
        for side in range(2):
            for p in range(parts):
                total = back_in[m, p, side].astype(F32)
                for q in range(1, chips):
                    total = total + back_in[m, p, 2 * q + side].astype(F32)
                pieces.append(total)
        back = jnp.concatenate(pieces, axis=1)
        arrived_f = arrived[m].astype(F32)
        scale = scales[m][:, :1]
        weighted = back * gains[...]
        mean_term = jnp.mean(weighted * arrived_f, axis=-1, keepdims=True)
        total = up_in[m].astype(F32) + scale * (weighted - arrived_f * scale * scale * mean_term)
        up_out[m] = total.astype(BF16)
        for q in range(chips):
            slope = up_out[m, :, part(q)].astype(F32) * hidden[m, :, part(q)]
            slopes[0, m, q] = slope.astype(BF16)
        send_slopes(0, m, before, True)

        @pl.when(section > 1)
        def _():
            remote(
                up_out.at[m], up_in.at[m], side_send.at[1, m], side_recv.at[1, m], before, me
            ).start()

    FR, FC, TR, BC, BR, TN, NO = range(7)

    def code(kind, m=0, chain=0):
        return kind * 4 + m * 2 + chain

    plain = [
        [(FR, 0), (FC, 0, 0), (FC, 0, 1), (FR, 1), (FC, 1, 0), (FC, 1, 1),
         (TN, 0), (TN, 1), (BC, 0, 0), (BR, 0), (BC, 0, 1), (BC, 1, 0), (BR, 1), (BC, 1, 1)],
        [(FC, 0, 0), (FR, 0), (FC, 0, 1), (FC, 1, 0), (FR, 1), (FC, 1, 1),
         (TN, 0), (TN, 1), (BC, 0, 0), (BC, 0, 1), (BR, 0), (BC, 1, 0), (BC, 1, 1), (BR, 1)],
    ]
    turning = [
        [(FR, 0), (FC, 0, 0), (TR, 0), (FC, 0, 1), (FR, 1), (BC, 0, 0), (FC, 1, 0),
         (BC, 0, 1), (BR, 0), (TR, 1), (FC, 1, 1), (BC, 1, 0), (BR, 1), (BC, 1, 1), (TN, 0), (TN, 1)],
        [(FC, 0, 0), (FR, 0), (FC, 0, 1), (BC, 0, 0), (TR, 0), (FC, 1, 0), (FR, 1),
         (BC, 0, 1), (FC, 1, 1), (BC, 1, 0), (BR, 0), (TR, 1), (BC, 1, 1), (BR, 1), (TN, 0), (TN, 1)],
    ]
    orders = [
        [[code(*entry) for entry in order + [(NO,)] * (16 - len(order))] for order in pair]
        for pair in (plain, turning)
    ]

    def run(t, carry):
        def chosen(order):
            value = order[0]
            for i in range(1, len(order)):
                value = jnp.where(t == i, order[i], value)
            return value

        now = jnp.where(
            last,
            jnp.where(core == 0, chosen(orders[1][0]), chosen(orders[1][1])),
            jnp.where(core == 0, chosen(orders[0][0]), chosen(orders[0][1])),
        )
        kind = lax.div(now, 4)
        m = lax.rem(lax.div(now, 2), 2)
        chain = lax.rem(now, 2)
        pl.when(kind == FR)(lambda: forward_rows(m))
        pl.when(kind == FC)(lambda: forward_columns(m, chain))
        pl.when(kind == TR)(lambda: turn_rows(m))
        pl.when(kind == BC)(lambda: backward_columns(m, chain))
        pl.when((kind == BR) & jnp.logical_not(first))(lambda: backward_rows(m))
        pl.when(kind == TN)(lambda: turn_normed(m))
        return carry

    lax.fori_loop(0, 16, run, 0)

    own_gains = jnp.where(core == 0, gains[:, :half], gains[:, half:])
    gain_row[...] = jnp.sum(gain_sum[...], axis=0, keepdims=True) / own_gains

    def gain_send(step, carry):
        other = far_device(step)
        remote(
            gain_row, gain_in.at[me], gain_sem.at[0], gain_sem.at[1], section, other
        ).start()
        return carry

    lax.fori_loop(0, groups - 1, gain_send, 0)
    pltpu.make_async_copy(gain_row, gain_in.at[me], gain_sem.at[1]).start()

    arrived_copy = pltpu.make_async_copy(arrived, arrived_out, gain_sem.at[2])
    arrived_copy.start()
    weight_share.wait_send()
    for m in range(micro):
        for p in range(parts):
            await_bytes(back_in.at[m, p, 0 : groups - 1], gather_send.at[m])
        for chain in range(2):

            @pl.when(last & (core == chain))
            def _(m=m, chain=chain):
                await_bytes(pout.at[m, chain, 0 : chips - 1], part_send.at[m, chain])

            @pl.when(jnp.logical_not(last & (core == chain)))
            def _(m=m, chain=chain):
                await_bytes(pout.at[m, chain], part_send.at[m, chain])

            @pl.when(jnp.logical_not(first) & (core == chain))
            def _(m=m, chain=chain):
                await_bytes(back_out.at[m, chain, :, 0 : chips - 1], back_send.at[m, chain])

            @pl.when(jnp.logical_not(first) & (core != chain))
            def _(m=m, chain=chain):
                await_bytes(back_out.at[m, chain], back_send.at[m, chain])

            slope_copy(m, chain).wait()

        keep_share(m).wait()
        keep_own(m).wait()

        @pl.when(last)
        def _(m=m):
            await_bytes(pin.at[1, m, 0 : groups - 1], slope_send.at[1, m])

        @pl.when(jnp.logical_not(first))
        def _(m=m):
            await_bytes(pin.at[0, m], slope_send.at[0, m])

        @pl.when(section > 1)
        def _(m=m):
            await_bytes(up_out.at[m], side_send.at[1, m])

        @pl.when(jnp.logical_not(last))
        def _(m=m):
            await_bytes(arrived.at[m], side_send.at[0, m])

    await_bytes(gain_in, gain_sem.at[1])
    for side in range(2):
        total = gain_in[side]
        for q in range(1, chips):
            total = total + gain_in[2 * q + side]
        gain_full[:, side * half : (side + 1) * half] = total
    await_bytes(gain_in.at[0 : groups - 1], gain_sem.at[0])
    gain_copy = pltpu.make_async_copy(gain_full, gain_out, gain_sem.at[3])
    gain_copy.start()
    arrived_copy.wait()
    gain_copy.wait()


def on_device(sections, groups, acts_in, weights, gains, stored, sample_ids, cotangent):
    micro, seg_rows, width = acts_in.shape
    own_cols = weights.shape[2]
    half = width // 2
    chip_cols = 2 * own_cols
    chips = groups // 2
    rows = chips * seg_rows
    parts = 3
    span = half // parts
    anywhere = pl.BlockSpec(memory_space=pl.ANY)
    smem = pl.BlockSpec(memory_space=pltpu.SMEM)
    dma = pltpu.SemaphoreType.DMA
    arrived, normed, slope, gain = pl.pallas_call(
        functools.partial(relay, sections, groups),
        out_shape=(
            jax.ShapeDtypeStruct((micro, seg_rows, width), BF16),
            jax.ShapeDtypeStruct((width, micro * 2 * rows), BF16),
            jax.ShapeDtypeStruct((micro * 2 * rows, own_cols), BF16),
            jax.ShapeDtypeStruct((1, width), F32),
        ),
        in_specs=[smem] + [anywhere] * 5,
        out_specs=(anywhere,) * 4,
        scratch_shapes=[
            pltpu.VMEM((micro, seg_rows, width), BF16),
            pltpu.VMEM((1, width), F32),
            pltpu.VMEM(stored.shape, BF16),
            pltpu.VMEM((micro, seg_rows, width), BF16),
            pltpu.VMEM((half, chip_cols), BF16),
            pltpu.VMEM((micro, parts, 2, seg_rows, span), BF16),
            pltpu.VMEM((micro, 2, parts, chips, seg_rows, span), BF16),
            pltpu.VMEM((micro, 2, rows, half), BF16),
            pltpu.VMEM((micro, 2, chips, seg_rows, chip_cols), BF16),
            pltpu.VMEM((2, micro, groups, seg_rows, chip_cols), BF16),
            pltpu.VMEM((micro, seg_rows, width), F32),
            pltpu.VMEM((seg_rows, width), F32),
            pltpu.VMEM((micro, seg_rows, width), BF16),
            pltpu.VMEM((micro, seg_rows, width), BF16),
            pltpu.VMEM((2, micro, chips, seg_rows, chip_cols), BF16),
            pltpu.VMEM((micro, 2, chips, seg_rows, chip_cols), BF16),
            pltpu.VMEM((micro, 2, rows, chip_cols), BF16),
            pltpu.VMEM((micro, 2, parts, chips, seg_rows, span), BF16),
            pltpu.VMEM((micro, parts, groups, seg_rows, span), BF16),
            pltpu.VMEM((micro, seg_rows, width), BF16),
            pltpu.VMEM((micro, seg_rows, width), BF16),
            pltpu.VMEM((micro, seg_rows, 128), F32),
            pltpu.VMEM((micro, half, 2 * rows), BF16),
            pltpu.VMEM((rows, chip_cols), F32),
            pltpu.VMEM((seg_rows, half), F32),
            pltpu.VMEM((1, half), F32),
            pltpu.VMEM((groups, 1, half), F32),
            pltpu.VMEM((1, width), F32),
            dma((4,)),
            dma((3,)),
            dma((micro,)),
            dma((micro, 2, parts)),
            dma((micro, 2)),
            dma((2, micro)),
            dma((2, micro)),
            dma((micro, 2)),
            dma((micro, 2)),
            dma((micro,)),
            dma((2, micro)),
            dma((2, micro)),
            dma((micro,)),
            dma((micro,)),
            dma((2, micro, 2)),
            dma((4,)),
        ],
        compiler_params=pltpu.CompilerParams(
            collective_id=0, has_side_effects=True, vmem_limit_bytes=60 * 1024 * 1024
        ),
    )(sample_ids, acts_in, weights, gains, stored, cotangent)

    block_k = 512
    blocks = width // block_k
    slot_count = stored.shape[1]

    def finish(
        ids_ref, normed_ref, slope_ref, stored_ref, arrived_ref, gain_ref,
        kept_ref, grad_ref, total_ref,
        normed_buf, slope_buf, kept_buf, arrived_buf, grad_buf, in_sem, out_sem, side_sem,
    ):
        side = [
            pltpu.make_async_copy(slope_ref, slope_buf, side_sem.at[0]),
            pltpu.make_async_copy(stored_ref, kept_buf, side_sem.at[1]),
            pltpu.make_async_copy(arrived_ref, arrived_buf, side_sem.at[2]),
            pltpu.make_async_copy(gain_ref, total_ref, side_sem.at[3]),
        ]
        places = [pl.ds(b * block_k, block_k) for b in range(blocks)]
        takes = [
            pltpu.make_async_copy(normed_ref.at[place], normed_buf.at[place], in_sem.at[b])
            for b, place in enumerate(places)
        ]
        gives = [
            pltpu.make_async_copy(grad_buf.at[place], grad_ref.at[0, place], out_sem.at[b])
            for b, place in enumerate(places)
        ]
        side[0].start()
        for take in takes:
            take.start()
        for copy in side[1:]:
            copy.start()
        side[0].wait()
        for place, take, give in zip(places, takes, gives):
            take.wait()
            grad_buf[place] = jnp.dot(
                normed_buf[place], slope_buf[...], preferred_element_type=F32
            )
            give.start()
        side[1].wait()
        side[2].wait()
        for m in range(micro):
            slot = ids_ref[m, 0] - lax.axis_index("dp") * slot_count
            kept_buf[0, jnp.clip(slot, 0, slot_count - 1)] = arrived_buf[m]
        kept_copy = pltpu.make_async_copy(kept_buf, kept_ref, side_sem.at[4])
        kept_copy.start()
        side[3].wait()
        kept_copy.wait()
        for give in gives:
            give.wait()

    kept, grad, gain = pl.pallas_call(
        finish,
        out_shape=(
            jax.ShapeDtypeStruct(stored.shape, BF16),
            jax.ShapeDtypeStruct((1, width, own_cols), F32),
            jax.ShapeDtypeStruct((1, width), F32),
        ),
        in_specs=[smem] + [anywhere] * 5,
        out_specs=(anywhere,) * 3,
        scratch_shapes=[
            pltpu.VMEM(normed.shape, BF16),
            pltpu.VMEM(slope.shape, BF16),
            pltpu.VMEM(stored.shape, BF16),
            pltpu.VMEM(arrived.shape, BF16),
            pltpu.VMEM((width, own_cols), F32),
            dma((blocks,)),
            dma((blocks,)),
            dma((5,)),
        ],
        compiler_params=pltpu.CompilerParams(vmem_limit_bytes=60 * 1024 * 1024),
    )(sample_ids, normed, slope, stored, arrived, gain)
    return (kept, grad, gain)


def solution(mesh):
    placed = (
        P(None, "dp", None),
        P("section", None, "dp"),
        P("section", None),
        P("section", "dp", None, None),
        P(None, "dp"),
        P(None, "dp", None),
    )
    return jax.shard_map(
        functools.partial(on_device, mesh.shape["section"], mesh.shape["dp"]),
        mesh=mesh,
        in_specs=placed,
        out_specs=(P("section", "dp", None, None), P("section", None, "dp"), P("section", None)),
        check_vma=False,
    )
```

profile of v0, /device:TPU:1, one launch (start us, length us, event | category | flops | bytes accessed | tf_op | source)
XLA Modules:
  0.0 277.7 jit_solution(13338902594813010114)
XLA Ops:
  0.6 1.3 copy.10.ids.ids_ref
  2.0 268.6 %shard_map.85 = (bf16[2,8,6144]{2,1,0:T(8,128)(2,1)}, bf16[6144,256]{1,0:T(8,128)(2,1)}, bf16[256,384]{1,0:T(8,128)(2,1)}, f32[1,6144]{1,0:T(1,128)}) custom-call(s32[2,1]{1,0:T(2,128)} %copy.10.ids.ids_ref, bf16[2,8,6144]{2,1,0:T(8,128)(2,1)} %acts_hbm.1, bf16[1,6144,384]{2,1,0:T(8,128)(2,1)} %weights.1, f32[1,6144]{1,0:T(1,128)} %gains_hbm.1, ...), custom_call_target="tpu_custom_call" | custom-call | tf_op jit(solution)/shard_map/pallas_call | solution.py:598
  270.6 7.1 %shard_map.86 = (bf16[1,4,8,6144]{3,2,1,0:T(8,128)(2,1)}, f32[1,6144,384]{2,1,0:T(8,128)}, f32[1,6144]{1,0:T(1,128)}) custom-call(s32[2,1]{1,0:T(2,128)} %copy.10.ids.ids_ref, bf16[6144,256]{1,0:T(8,128)(2,1)} %get-tuple-element.7.normed_ref, bf16[256,384]{1,0:T(8,128)(2,1)} %get-tuple-element.8.slope_ref, bf16[1,4,8,6144]{3,2,1,0:T(8,128)(2,1)} %stored_ref.1, ...), custom_call_target="tpu_custom_call" | custom-call | tf_op jit(solution)/shard_map/pallas_call | solution.py:707
where the time goes:
time: 278 us
  Pallas kernels  276 us (99%)
    pallas_call x1, Pallas kernels, on_device(): pl.pallas_call(functools.partial(relay, sections, groups), out_shape=(jax...  269 us
    pallas_call x1, Pallas kernels, on_device(): pl.pallas_call(finish, out_shape=(jax.ShapeDtypeStruct(stored.shape, BF16...  7.12 us

commit v1 on v0

v1 whole, which is shorter than its diff:
```python
import functools

import jax
import jax.numpy as jnp
from jax import lax
from jax.experimental import pallas as pl
from jax.experimental.pallas import tpu as pltpu
from jax.sharding import PartitionSpec as P

MESH = pl.DeviceIdType.MESH
F32 = jnp.float32
BF16 = jnp.bfloat16

clip_limit = 1.0
epsilon = 1e-05
gelu_coeff = 0.7978845608028654


def gelu_value(values):
    inner = gelu_coeff * (values + 0.044715 * values * values * values)
    return 0.5 * values * (1.0 + jnp.tanh(inner))


def gelu_slope(values):
    tangent = jnp.tanh(gelu_coeff * (values + 0.044715 * values * values * values))
    return 0.5 * (1.0 + tangent) + 0.5 * values * (1.0 - tangent * tangent) * gelu_coeff * (
        1.0 + 0.134145 * values * values
    )


part_count = 2
step_b = 256
stagger_us, gather_us, turn_us, slope_us, back_us = 3.5, 5.5, 5.5, 4.6, 6.4


def make_order(micro, turning, side):
    FR, FC, TR, BC, BR, TN = range(6)
    events = []
    for k in range(4 * micro):
        start = stagger_us * k
        back = start + gather_us + turn_us + slope_us if turning else start + 1000.0
        events.append((start + gather_us, FC * 8 + k))
        events.append((back, BC * 8 + k))
        if k % 2 == side:
            events.append((start, FR * 8 + k))
            events.append((back + back_us, BR * 8 + k))
            if turning:
                events.append((start + gather_us + turn_us, TR * 8 + k))
    for m in range(micro):
        events.append((2000.0 if turning else 500.0, TN * 8 + 4 * m))
    return [entry for _, entry in sorted(events)]


def relay(
    sections,
    groups,
    ids,
    acts_hbm,
    weights,
    gains_hbm,
    stored_hbm,
    cotangent_hbm,
    arrived_out,
    normed_out,
    slope_out,
    gain_out,
    acts,
    gains,
    stored,
    cotangent,
    acts_p,
    before_p,
    cotangent_p,
    gains_p,
    wbuf,
    nbuf,
    gbuf,
    xbuf,
    products,
    pout,
    pin,
    hidden,
    incoming,
    arrived,
    arrived_whole,
    arr_in,
    slopes,
    slope_in,
    ybuf,
    own_slope,
    back_out,
    back_in,
    up_in,
    up_out,
    scales,
    xturned,
    gain_sum,
    gain_row,
    gain_in,
    gain_full,
    load_sem,
    w_sem,
    gather_send,
    gather_recv,
    part_send,
    part_recv,
    slope_send,
    slope_recv,
    back_send,
    back_recv,
    side_send,
    side_recv,
    keep_send,
    keep_recv,
    keep_sem,
    copy_sem,
    gain_sem,
    stagger,
):
    micro, seg_rows, width = acts.shape
    half = width // 2
    fold = half // 2
    own_cols = weights.shape[2]
    chip_cols = 2 * own_cols
    chips = groups // 2
    quarter = chips // 2
    rows = chips * seg_rows
    slot_count = stored.shape[1]
    sets = 2 * micro
    parts = gbuf.shape[2]
    span = fold // parts
    section = lax.axis_index("section")
    me = lax.axis_index("dp")
    core = lax.rem(me, 2)
    chip = lax.div(me, 2)
    sibling = me + 1 - 2 * core
    first = section == 0
    last = section == sections - 1
    after = lax.rem(section + 1, sections)
    before = lax.rem(section + sections - 1, sections)
    z_count = groups // 4
    z_pos = lax.div(me, 4)
    x_pos = lax.rem(chip, 2)

    loads = [
        pltpu.make_async_copy(source, target, load_sem.at[i])
        for i, (source, target) in enumerate(
            (
                (acts_hbm, acts),
                (stored_hbm, stored),
                (gains_hbm, gains),
                (cotangent_hbm, cotangent),
            )
        )
    ]
    for load in loads:
        load.start()
    own_place = pl.ds(pl.multiple_of(core * own_cols, 128), own_cols)

    def weight_pieces(side):
        for q in range(quarter):
            for h in range(2):
                yield (
                    weights.at[
                        0, pl.ds(side * half + q * chip_cols + h * own_cols, own_cols), :
                    ],
                    wbuf.at[h, q * own_cols : (q + 1) * own_cols, own_place],
                )

    for source, target in weight_pieces(core):
        pltpu.make_async_copy(source, target, w_sem.at[2]).start()

    barrier = pltpu.get_barrier_semaphore()

    def greet(step, carry):
        other = lax.rem(me + step, groups)
        for there in (after, before):
            pl.semaphore_signal(
                barrier, inc=1, device_id={"section": there, "dp": other}, device_id_type=MESH
            )

        @pl.when(step > 0)
        def _():
            pl.semaphore_signal(
                barrier, inc=1, device_id={"section": section, "dp": other}, device_id_type=MESH
            )

        return carry

    lax.fori_loop(0, groups, greet, 0)

    def part(q):
        return slice(q * own_cols, (q + 1) * own_cols)

    def low_rows(shape):
        return lax.broadcasted_iota(jnp.int32, shape, len(shape) - 2) < 4

    def turned(value):
        return pltpu.roll(value, 4, axis=value.ndim - 2)

    def columns(q, h):
        start = q * chip_cols + h * own_cols
        return slice(start, start + own_cols)

    def pack(value, target, index):
        for q in range(chips):
            left, right = value[:, columns(q, 0)], value[:, columns(q, 1)]
            low = low_rows(left.shape)
            target[index, :, part(q)] = jnp.where(low, left, turned(right)).astype(target.dtype)
            target[index + 1, :, part(q)] = jnp.where(low, turned(left), right).astype(
                target.dtype
            )

    def unpack(one, two):
        low = low_rows(one.shape)
        return jnp.where(low, one, turned(two)), jnp.where(low, turned(one), two)

    for load in loads:
        load.wait()
    for q in range(chips):
        left = jnp.broadcast_to(gains[:, columns(q, 0)], (seg_rows, own_cols))
        right = jnp.broadcast_to(gains[:, columns(q, 1)], (seg_rows, own_cols))
        gains_p[:, part(q)] = jnp.where(low_rows(left.shape), left, right)
    for m in range(micro):
        slot = jnp.clip(ids[m, 0] - me * slot_count, 0, slot_count - 1)
        pack(acts[m].astype(F32), acts_p, 2 * m)
        pack(stored[0, slot].astype(F32), before_p, 2 * m)
        pack(cotangent[m].astype(F32), cotangent_p, 2 * m)
    gain_sum[...] = jnp.zeros_like(gain_sum)
    pl.semaphore_wait(barrier, 3 * groups - 1)

    def remote(source, target, send, recv, there, other):
        return pltpu.make_async_remote_copy(
            src_ref=source,
            dst_ref=target,
            send_sem=send,
            recv_sem=recv,
            device_id={"section": there, "dp": other},
            device_id_type=MESH,
        )

    for source, target in weight_pieces(1 - core):
        remote(source, target, w_sem.at[0], w_sem.at[1], section, sibling).start()

    def far_z(i):
        away = jnp.where(i == 3, 0, jnp.where(i == 0, 2, 2 * i - 1))
        return lax.rem(z_pos + away, z_count)

    def far_device(i):
        x = lax.rem(x_pos + 1 - lax.rem(lax.div(i, 2), 2), 2)
        return far_z(lax.div(i, 4)) * 4 + x * 2 + lax.rem(core + 1 - lax.rem(i, 2), 2)

    def far_chip(i):
        return far_z(lax.div(i, 2)) * 2 + lax.rem(x_pos + 1 - lax.rem(i, 2), 2)

    def await_bytes(ref, sem):
        pltpu.make_async_copy(ref, ref, sem).wait()

    def row_mean(value):
        total = jnp.broadcast_to(jnp.sum(value, axis=-1, keepdims=True), (seg_rows, 128))
        return ((total + turned(total)) / width)[:, :1]

    def turned_place(m):
        wide = 2 * rows
        return (
            pl.ds(pl.multiple_of(core * half, half), half),
            pl.ds(pl.multiple_of(m * wide, wide), wide),
        )

    def keep_share(m):
        return remote(
            xturned.at[m],
            normed_out.at[turned_place(m)],
            keep_send.at[m],
            keep_recv.at[m],
            section,
            sibling,
        )

    def keep_own(m):
        return pltpu.make_async_copy(xturned.at[m], normed_out.at[turned_place(m)], keep_sem.at[m])

    def turn_normed(m):
        for q in range(quarter):
            p, start = (q * own_cols) // span, (q * own_cols) % span
            sides = [[], []]
            for chain in range(2):
                one, two = (
                    gbuf[2 * m + u, chain, p, :, :, start : start + own_cols].astype(F32)
                    for u in range(2)
                )
                for h, whole in enumerate(unpack(one, two)):
                    sides[h].append(whole.reshape(rows, own_cols))
            for h in range(2):
                piece = jnp.transpose(jnp.concatenate(sides[h], axis=0))
                xturned[m, columns(q, h), :] = piece.astype(BF16)
        keep_share(m).start()
        keep_own(m).start()

    def slope_copy(m, chain):
        return pltpu.make_async_copy(
            own_slope.at[m, chain],
            slope_out.at[pl.ds(pl.multiple_of((m * 2 + chain) * rows, rows), rows), :],
            copy_sem.at[m, chain],
        )

    def send_slopes(kind, e, there, remote_own):
        def send(step, carry):
            other = far_device(step)
            remote(
                slopes.at[kind, e, lax.div(other, 2)],
                slope_in.at[e, core, chip],
                slope_send.at[kind, e],
                slope_recv.at[e, core],
                there,
                other,
            ).start()
            return carry

        if remote_own:
            lax.fori_loop(0, groups, send, 0)
        else:
            lax.fori_loop(0, groups - 1, send, 0)
            pltpu.make_async_copy(
                slopes.at[kind, e, chip], slope_in.at[e, core, chip], slope_recv.at[e, core]
            ).start()

    def summed_parts(kind, e, q):
        return pin[kind, e, 2 * q].astype(F32) + pin[kind, e, 2 * q + 1].astype(F32)

    def forward_rows(e):
        @pl.when(first & (e == 0) & (core == 1))
        def _():
            pl.semaphore_wait(stagger, 1)

        @pl.when(first)
        def _():
            incoming[...] = acts_p[e]

        @pl.when(jnp.logical_not(first))
        def _():
            await_bytes(arr_in.at[e], side_recv.at[0, e])
            await_bytes(pin.at[0, e], part_recv.at[0, e])
            for q in range(chips):
                value = summed_parts(0, e, q)
                hidden[e, :, part(q)] = value
                total = arr_in[e, :, part(q)].astype(F32) + gelu_value(value)
                incoming[:, part(q)] = total.astype(BF16).astype(F32)

        previous = before_p[e]
        moved = jnp.clip(incoming[...] - previous, -clip_limit, clip_limit)
        arrived_now = (previous + moved).astype(BF16)
        arrived[e] = arrived_now
        arrived_f = arrived_now.astype(F32)
        scale = lax.rsqrt(row_mean(arrived_f * arrived_f) + epsilon)
        scales[e] = jnp.broadcast_to(scale, (seg_rows, 128))
        normed = (arrived_f * scale * gains_p[...]).astype(BF16)
        for side in range(2):
            for p in range(parts):
                start = side * fold + p * span
                nbuf[e, p, side] = normed[:, start : start + span]
        for p in range(parts):

            def send(step, carry, p=p):
                other = far_device(step)
                remote(
                    nbuf.at[e, p, lax.rem(other, 2)],
                    gbuf.at[e, core, p, chip],
                    gather_send.at[e],
                    gather_recv.at[e, core, p],
                    section,
                    other,
                ).start()
                return carry

            lax.fori_loop(0, groups - 1, send, 0)
            pltpu.make_async_copy(
                nbuf.at[e, p, core], gbuf.at[e, core, p, chip], gather_recv.at[e, core, p]
            ).start()

        @pl.when(jnp.logical_not(last))
        def _():
            remote(
                arrived.at[e], arr_in.at[e], side_send.at[0, e], side_recv.at[0, e], after, me
            ).start()

        @pl.when(jnp.logical_not(first))
        def _():
            for q in range(chips):
                hidden[e, :, part(q)] = gelu_slope(hidden[e, :, part(q)])

    def forward_columns(e, chain):
        @pl.when((e == 0) & (chain == 0))
        def _():
            await_bytes(wbuf.at[:, :, own_place], w_sem.at[2])
            await_bytes(wbuf.at[:, :, own_place], w_sem.at[1])

        for p in range(parts):
            await_bytes(gbuf.at[e, chain, p], gather_recv.at[e, chain, p])
            if p == 0:

                @pl.when(first & (e == 0) & (chain == 0) & (core == 0))
                def _():
                    pl.semaphore_signal(
                        stagger, inc=1, device_id={"dp": sibling}, device_id_type=MESH
                    )

            base = p * span
            piece = gbuf[e, chain, p].astype(F32).reshape(rows, span)
            xbuf[:, base : base + span] = piece.astype(BF16)
            for h in range(2):
                for c in range(0, chip_cols, 256):
                    product = jnp.dot(
                        xbuf[:, base : base + span],
                        wbuf[h, base : base + span, c : c + 256],
                        preferred_element_type=F32,
                    )
                    if p > 0:
                        product = product + products[h, :, c : c + 256]
                    products[h, :, c : c + 256] = product
        shape = (chips, seg_rows, own_cols)
        left = products[0, :, :own_cols].reshape(shape) + turned(
            products[1, :, :own_cols].reshape(shape)
        )
        right = (
            turned(products[0, :, own_cols:].reshape(shape))
            + products[1, :, own_cols:].reshape(shape)
        )
        pout[e, chain] = jnp.where(low_rows(shape), left, right).astype(BF16)

        def send(step, carry):
            q = far_chip(step)
            other = 2 * q + chain

            @pl.when(jnp.logical_not(last))
            def _():
                remote(
                    pout.at[e, chain, q],
                    pin.at[0, e, me],
                    part_send.at[e, chain],
                    part_recv.at[0, e],
                    after,
                    other,
                ).start()

            @pl.when(last & (other != me))
            def _():
                remote(
                    pout.at[e, chain, q],
                    pin.at[1, e, me],
                    part_send.at[e, chain],
                    part_recv.at[1, e],
                    section,
                    other,
                ).start()

            return carry

        lax.fori_loop(0, chips, send, 0)

        @pl.when(last & (core == chain))
        def _():
            pltpu.make_async_copy(
                pout.at[e, chain, chip], pin.at[1, e, me], part_recv.at[1, e]
            ).start()

    def turn_rows(e):
        await_bytes(pin.at[1, e], part_recv.at[1, e])
        for q in range(chips):
            slope = cotangent_p[e, :, part(q)].astype(F32) * gelu_slope(summed_parts(1, e, q))
            slopes[1, e, q] = slope.astype(BF16)
        send_slopes(1, e, section, False)

    def backward_columns(e, chain):
        await_bytes(slope_in.at[e, chain], slope_recv.at[e, chain])
        ybuf[...] = slope_in[e, chain].astype(F32).reshape(rows, own_cols).astype(BF16)
        for p in range(parts):
            for k in range(0, span, step_b):
                start = p * span + k
                shape = (chips, seg_rows, step_b)
                terms = [
                    [
                        lax.dot_general(
                            ybuf[...],
                            wbuf[h, start : start + step_b, s * own_cols : (s + 1) * own_cols],
                            (((1,), (1,)), ((), ())),
                            preferred_element_type=F32,
                        ).reshape(shape)
                        for s in range(2)
                    ]
                    for h in range(2)
                ]
                left = terms[0][0] + turned(terms[0][1])
                right = turned(terms[1][0]) + terms[1][1]
                back_out[e, chain, p, :, :, k : k + step_b] = jnp.where(
                    low_rows(shape), left, right
                ).astype(BF16)

            def send(step, carry, p=p):
                q = far_chip(step)
                other = 2 * q + chain

                @pl.when(other != me)
                def _():
                    remote(
                        back_out.at[e, chain, p, q],
                        back_in.at[e, p, me],
                        back_send.at[e, chain],
                        back_recv.at[e],
                        section,
                        other,
                    ).start()

                return carry

            @pl.when(jnp.logical_not(first))
            def _(p=p, send=send):
                lax.fori_loop(0, chips, send, 0)

            @pl.when(jnp.logical_not(first) & (core == chain))
            def _(p=p):
                pltpu.make_async_copy(
                    back_out.at[e, chain, p, chip], back_in.at[e, p, me], back_recv.at[e]
                ).start()

        for p in range(parts):
            term = back_out[e, chain, p].astype(F32) * gbuf[e, chain, p].astype(F32)
            gain_sum[:, p * span : (p + 1) * span] += jnp.sum(term, axis=0)

        @pl.when(lax.rem(e, 2) == 1)
        def _():
            m = lax.div(e, 2)
            left, right = unpack(
                slope_in[e - 1, chain].astype(F32), slope_in[e, chain].astype(F32)
            )
            mine = jnp.where(core == 0, left, right).reshape(rows, own_cols)
            own_slope[m, chain] = mine.astype(BF16)
            slope_copy(m, chain).start()

    def backward_rows(e):
        @pl.when(last)
        def _():
            up_in[e] = cotangent_p[e]

        @pl.when(jnp.logical_not(last))
        def _():
            await_bytes(up_in.at[e], side_recv.at[1, e])

        await_bytes(back_in.at[e], back_recv.at[e])
        pieces = []
        for side in range(2):
            for p in range(parts):
                total = back_in[e, p, side].astype(F32)
                for q in range(1, chips):
                    total = total + back_in[e, p, 2 * q + side].astype(F32)
                pieces.append(total)
        back = jnp.concatenate(pieces, axis=1)
        arrived_f = arrived[e].astype(F32)
        scale = scales[e][:, :1]
        weighted = back * gains_p[...]
        mean_term = row_mean(weighted * arrived_f)
        total = up_in[e].astype(F32) + scale * (weighted - arrived_f * scale * scale * mean_term)
        up_out[e] = total.astype(BF16)
        for q in range(chips):
            slope = up_out[e, :, part(q)].astype(F32) * hidden[e, :, part(q)]
            slopes[0, e, q] = slope.astype(BF16)
        send_slopes(0, e, before, True)

        @pl.when(section > 1)
        def _():
            remote(
                up_out.at[e], up_in.at[e], side_send.at[1, e], side_recv.at[1, e], before, me
            ).start()

    FR, FC, TR, BC, BR, TN, NO = range(7)
    orders = [[make_order(micro, where, side) for side in range(2)] for where in range(2)]
    length = max(len(order) for pair in orders for order in pair)
    for pair in orders:
        for order in pair:
            order += [NO * 8] * (length - len(order))

    def run(t, carry):
        now = NO * 8
        for i in range(length):
            here = jnp.where(
                last,
                jnp.where(core == 0, orders[1][0][i], orders[1][1][i]),
                jnp.where(core == 0, orders[0][0][i], orders[0][1][i]),
            )
            now = jnp.where(t == i, here, now)
        kind = lax.div(now, 8)
        e = lax.rem(lax.div(now, 2), sets)
        chain = lax.rem(now, 2)
        pl.when(kind == FR)(lambda: forward_rows(e))
        pl.when(kind == FC)(lambda: forward_columns(e, chain))
        pl.when(kind == TR)(lambda: turn_rows(e))
        pl.when(kind == BC)(lambda: backward_columns(e, chain))
        pl.when((kind == BR) & jnp.logical_not(first))(lambda: backward_rows(e))
        pl.when(kind == TN)(lambda: turn_normed(lax.div(e, 2)))
        return carry

    lax.fori_loop(0, length, run, 0)

    low = low_rows(gain_sum.shape)
    sums = gain_sum[...]
    left = jnp.sum(jnp.where(low, sums, 0.0), axis=0, keepdims=True)
    right = jnp.sum(jnp.where(low, 0.0, sums), axis=0, keepdims=True)
    own_gains = jnp.where(core == 0, gains[:, :half], gains[:, half:])
    for q in range(quarter):
        for h, value in enumerate((left, right)):
            gain_row[:, columns(q, h)] = value[:, part(q)] / own_gains[:, columns(q, h)]

    def gain_send(step, carry):
        other = far_device(step)
        remote(
            gain_row, gain_in.at[me], gain_sem.at[0], gain_sem.at[1], section, other
        ).start()
        return carry

    lax.fori_loop(0, groups - 1, gain_send, 0)
    pltpu.make_async_copy(gain_row, gain_in.at[me], gain_sem.at[1]).start()

    for m in range(micro):
        for q in range(chips):
            wholes = unpack(
                arrived[2 * m, :, part(q)].astype(F32), arrived[2 * m + 1, :, part(q)].astype(F32)
            )
            for h, whole in enumerate(wholes):
                arrived_whole[m, :, columns(q, h)] = whole.astype(BF16)
    arrived_copy = pltpu.make_async_copy(arrived_whole, arrived_out, gain_sem.at[2])
    arrived_copy.start()
    await_bytes(wbuf.at[:, :, own_place], w_sem.at[0])
    for e in range(sets):
        for p in range(parts):
            await_bytes(back_in.at[e, p, 0 : groups - 1], gather_send.at[e])
        for chain in range(2):

            @pl.when(last & (core == chain))
            def _(e=e, chain=chain):
                await_bytes(pout.at[e, chain, 0 : chips - 1], part_send.at[e, chain])

            @pl.when(jnp.logical_not(last & (core == chain)))
            def _(e=e, chain=chain):
                await_bytes(pout.at[e, chain], part_send.at[e, chain])

            @pl.when(jnp.logical_not(first) & (core == chain))
            def _(e=e, chain=chain):
                await_bytes(back_out.at[e, chain, :, 0 : chips - 1], back_send.at[e, chain])

            @pl.when(jnp.logical_not(first) & (core != chain))
            def _(e=e, chain=chain):
                await_bytes(back_out.at[e, chain], back_send.at[e, chain])

        @pl.when(last)
        def _(e=e):
            await_bytes(pin.at[1, e, 0 : groups - 1], slope_send.at[1, e])

        @pl.when(jnp.logical_not(first))
        def _(e=e):
            await_bytes(pin.at[0, e], slope_send.at[0, e])

        @pl.when(section > 1)
        def _(e=e):
            await_bytes(up_out.at[e], side_send.at[1, e])

        @pl.when(jnp.logical_not(last))
        def _(e=e):
            await_bytes(arrived.at[e], side_send.at[0, e])

    for m in range(micro):
        for chain in range(2):
            slope_copy(m, chain).wait()
        keep_share(m).wait()
        keep_own(m).wait()

    await_bytes(gain_in, gain_sem.at[1])
    for side in range(2):
        total = gain_in[side]
        for q in range(1, chips):
            total = total + gain_in[2 * q + side]
        gain_full[:, side * half : (side + 1) * half] = total
    await_bytes(gain_in.at[0 : groups - 1], gain_sem.at[0])
    gain_copy = pltpu.make_async_copy(gain_full, gain_out, gain_sem.at[3])
    gain_copy.start()
    arrived_copy.wait()
    gain_copy.wait()


def on_device(sections, groups, acts_in, weights, gains, stored, sample_ids, cotangent):
    micro, seg_rows, width = acts_in.shape
    own_cols = weights.shape[2]
    half = width // 2
    fold = half // 2
    chip_cols = 2 * own_cols
    chips = groups // 2
    rows = chips * seg_rows
    sets = 2 * micro
    parts = part_count
    span = fold // parts
    anywhere = pl.BlockSpec(memory_space=pl.ANY)
    smem = pl.BlockSpec(memory_space=pltpu.SMEM)
    dma = pltpu.SemaphoreType.DMA
    arrived, normed, slope, gain = pl.pallas_call(
        functools.partial(relay, sections, groups),
        out_shape=(
            jax.ShapeDtypeStruct((micro, seg_rows, width), BF16),
            jax.ShapeDtypeStruct((width, micro * 2 * rows), BF16),
            jax.ShapeDtypeStruct((micro * 2 * rows, own_cols), BF16),
            jax.ShapeDtypeStruct((1, width), F32),
        ),
        in_specs=[smem] + [anywhere] * 5,
        out_specs=(anywhere,) * 4,
        scratch_shapes=[
            pltpu.VMEM((micro, seg_rows, width), BF16),
            pltpu.VMEM((1, width), F32),
            pltpu.VMEM(stored.shape, BF16),
            pltpu.VMEM((micro, seg_rows, width), BF16),
            pltpu.VMEM((sets, seg_rows, half), F32),
            pltpu.VMEM((sets, seg_rows, half), F32),
            pltpu.VMEM((sets, seg_rows, half), BF16),
            pltpu.VMEM((seg_rows, half), F32),
            pltpu.VMEM((2, fold, chip_cols), BF16),
            pltpu.VMEM((sets, parts, 2, seg_rows, span), BF16),
            pltpu.VMEM((sets, 2, parts, chips, seg_rows, span), BF16),
            pltpu.VMEM((rows, fold), BF16),
            pltpu.VMEM((2, rows, chip_cols), F32),
            pltpu.VMEM((sets, 2, chips, seg_rows, own_cols), BF16),
            pltpu.VMEM((2, sets, groups, seg_rows, own_cols), BF16),
            pltpu.VMEM((sets, seg_rows, half), F32),
            pltpu.VMEM((seg_rows, half), F32),
            pltpu.VMEM((sets, seg_rows, half), BF16),
            pltpu.VMEM((micro, seg_rows, width), BF16),
            pltpu.VMEM((sets, seg_rows, half), BF16),
            pltpu.VMEM((2, sets, chips, seg_rows, own_cols), BF16),
            pltpu.VMEM((sets, 2, chips, seg_rows, own_cols), BF16),
            pltpu.VMEM((rows, own_cols), BF16),
            pltpu.VMEM((micro, 2, rows, own_cols), BF16),
            pltpu.VMEM((sets, 2, parts, chips, seg_rows, span), BF16),
            pltpu.VMEM((sets, parts, groups, seg_rows, span), BF16),
            pltpu.VMEM((sets, seg_rows, half), BF16),
            pltpu.VMEM((sets, seg_rows, half), BF16),
            pltpu.VMEM((sets, seg_rows, 128), F32),
            pltpu.VMEM((micro, half, 2 * rows), BF16),
            pltpu.VMEM((seg_rows, fold), F32),
            pltpu.VMEM((1, half), F32),
            pltpu.VMEM((groups, 1, half), F32),
            pltpu.VMEM((1, width), F32),
            dma((4,)),
            dma((3,)),
            dma((sets,)),
            dma((sets, 2, parts)),
            dma((sets, 2)),
            dma((2, sets)),
            dma((2, sets)),
            dma((sets, 2)),
            dma((sets, 2)),
            dma((sets,)),
            dma((2, sets)),
            dma((2, sets)),
            dma((micro,)),
            dma((micro,)),
            dma((micro,)),
            dma((micro, 2)),
            dma((4,)),
            pltpu.SemaphoreType.REGULAR,
        ],
        compiler_params=pltpu.CompilerParams(
            collective_id=0, has_side_effects=True, vmem_limit_bytes=60 * 1024 * 1024
        ),
    )(sample_ids, acts_in, weights, gains, stored, cotangent)

    block_k = 512
    blocks = width // block_k
    slot_count = stored.shape[1]

    def finish(
        ids_ref, normed_ref, slope_ref, stored_ref, arrived_ref, gain_ref,
        kept_ref, grad_ref, total_ref,
        normed_buf, slope_buf, kept_buf, arrived_buf, grad_buf, in_sem, out_sem, side_sem,
    ):
        side = [
            pltpu.make_async_copy(slope_ref, slope_buf, side_sem.at[0]),
            pltpu.make_async_copy(stored_ref, kept_buf, side_sem.at[1]),
            pltpu.make_async_copy(arrived_ref, arrived_buf, side_sem.at[2]),
            pltpu.make_async_copy(gain_ref, total_ref, side_sem.at[3]),
        ]
        places = [pl.ds(b * block_k, block_k) for b in range(blocks)]
        takes = [
            pltpu.make_async_copy(normed_ref.at[place], normed_buf.at[place], in_sem.at[b])
            for b, place in enumerate(places)
        ]
        gives = [
            pltpu.make_async_copy(grad_buf.at[place], grad_ref.at[0, place], out_sem.at[b])
            for b, place in enumerate(places)
        ]
        side[0].start()
        for take in takes:
            take.start()
        for copy in side[1:]:
            copy.start()
        side[0].wait()
        for place, take, give in zip(places, takes, gives):
            take.wait()
            grad_buf[place] = jnp.dot(
                normed_buf[place], slope_buf[...], preferred_element_type=F32
            )
            give.start()
        side[1].wait()
        side[2].wait()
        for m in range(micro):
            slot = ids_ref[m, 0] - lax.axis_index("dp") * slot_count
            kept_buf[0, jnp.clip(slot, 0, slot_count - 1)] = arrived_buf[m]
        kept_copy = pltpu.make_async_copy(kept_buf, kept_ref, side_sem.at[4])
        kept_copy.start()
        side[3].wait()
        kept_copy.wait()
        for give in gives:
            give.wait()

    kept, grad, gain = pl.pallas_call(
        finish,
        out_shape=(
            jax.ShapeDtypeStruct(stored.shape, BF16),
            jax.ShapeDtypeStruct((1, width, own_cols), F32),
            jax.ShapeDtypeStruct((1, width), F32),
        ),
        in_specs=[smem] + [anywhere] * 5,
        out_specs=(anywhere,) * 3,
        scratch_shapes=[
            pltpu.VMEM(normed.shape, BF16),
            pltpu.VMEM(slope.shape, BF16),
            pltpu.VMEM(stored.shape, BF16),
            pltpu.VMEM(arrived.shape, BF16),
            pltpu.VMEM((width, own_cols), F32),
            dma((blocks,)),
            dma((blocks,)),
            dma((5,)),
        ],
        compiler_params=pltpu.CompilerParams(vmem_limit_bytes=60 * 1024 * 1024),
    )(sample_ids, normed, slope, stored, arrived, gain)
    return (kept, grad, gain)


def solution(mesh):
    placed = (
        P(None, "dp", None),
        P("section", None, "dp"),
        P("section", None),
        P("section", "dp", None, None),
        P(None, "dp"),
        P(None, "dp", None),
    )
    return jax.shard_map(
        functools.partial(on_device, mesh.shape["section"], mesh.shape["dp"]),
        mesh=mesh,
        in_specs=placed,
        out_specs=(P("section", "dp", None, None), P("section", None, "dp"), P("section", None)),
        check_vma=False,
    )
```

time: 278 us -> 241 us (0.87)
  Pallas kernels: 276 us -> 239 us
    pallas_call x1, Pallas kernels: 269 us -> 232 us  [on_device(): pl.pallas_call(functools.partial(relay, sections, groups), out_shape=(jax...]
where the time goes in v1:
time: 241 us
  Pallas kernels  239 us (99%)
    pallas_call x1, Pallas kernels, on_device(): pl.pallas_call(functools.partial(relay, sections, groups), out_shape=(jax...  232 us
    pallas_call x1, Pallas kernels, on_device(): pl.pallas_call(finish, out_shape=(jax.ShapeDtypeStruct(stored.shape, BF16...  7.12 us

profile of v1, /device:TPU:1, one launch (start us, length us, event | category | flops | bytes accessed | tf_op | source)
XLA Modules:
  0.0 241.0 jit_solution(16240512465182885319)
XLA Ops:
  0.6 1.3 copy.10.ids.ids_ref
  2.0 231.9 %shard_map.85 = (bf16[2,8,6144]{2,1,0:T(8,128)(2,1)}, bf16[6144,256]{1,0:T(8,128)(2,1)}, bf16[256,384]{1,0:T(8,128)(2,1)}, f32[1,6144]{1,0:T(1,128)}) custom-call(s32[2,1]{1,0:T(2,128)} %copy.10.ids.ids_ref, bf16[2,8,6144]{2,1,0:T(8,128)(2,1)} %acts_hbm.1, bf16[1,6144,384]{2,1,0:T(8,128)(2,1)} %weights.1, f32[1,6144]{1,0:T(1,128)} %gains_hbm.1, ...), custom_call_target="tpu_custom_call" | custom-call | tf_op jit(solution)/shard_map/pallas_call | solution.py:703
  233.9 7.1 %shard_map.86 = (bf16[1,4,8,6144]{3,2,1,0:T(8,128)(2,1)}, f32[1,6144,384]{2,1,0:T(8,128)}, f32[1,6144]{1,0:T(1,128)}) custom-call(s32[2,1]{1,0:T(2,128)} %copy.10.ids.ids_ref, bf16[6144,256]{1,0:T(8,128)(2,1)} %get-tuple-element.7.normed_ref, bf16[256,384]{1,0:T(8,128)(2,1)} %get-tuple-element.8.slope_ref, bf16[1,4,8,6144]{3,2,1,0:T(8,128)(2,1)} %stored_ref.1, ...), custom_call_target="tpu_custom_call" | custom-call | tf_op jit(solution)/shard_map/pallas_call | solution.py:820

commit v2 on v1

--- a/solution.py
+++ b/solution.py
@@ -28,24 +28,25 @@
     )
 
 
-part_count = 2
+gather_cuts = (0, 768, 1280, 1536)
+back_cuts = (0, 512, 1024, 1536)
 step_b = 256
-stagger_us, gather_us, turn_us, slope_us, back_us = 3.5, 5.5, 5.5, 4.6, 6.4
+plain_us = (3.5, 5.5, 2.8, 6.4, 0.0)
+turning_us = (3.5, 5.5, 1.4, 6.4, 0.0)
 
 
 def make_order(micro, turning, side):
-    FR, FC, TR, BC, BR, TN = range(6)
+    FR, FC, BC, BR, TN = range(5)
+    stagger_us, gather_us, pair_us, back_us, late_us = turning_us if turning else plain_us
     events = []
     for k in range(4 * micro):
         start = stagger_us * k
-        back = start + gather_us + turn_us + slope_us if turning else start + 1000.0
+        back = start + gather_us + pair_us if turning else start + 1000.0
         events.append((start + gather_us, FC * 8 + k))
         events.append((back, BC * 8 + k))
         if k % 2 == side:
-            events.append((start, FR * 8 + k))
+            events.append((start + (late_us if k >= 4 else 0.0), FR * 8 + k))
             events.append((back + back_us, BR * 8 + k))
-            if turning:
-                events.append((start + gather_us + turn_us, TR * 8 + k))
     for m in range(micro):
         events.append((2000.0 if turning else 500.0, TN * 8 + 4 * m))
     return [entry for _, entry in sorted(events)]
@@ -79,6 +80,7 @@
     products,
     pout,
     pin,
+    pair_in,
     hidden,
     incoming,
     arrived,
@@ -104,6 +106,7 @@
     gather_recv,
     part_send,
     part_recv,
+    pair_recv,
     slope_send,
     slope_recv,
     back_send,
@@ -127,8 +130,8 @@
     rows = chips * seg_rows
     slot_count = stored.shape[1]
     sets = 2 * micro
-    parts = gbuf.shape[2]
-    span = fold // parts
+    gather_parts = list(zip(gather_cuts[:-1], gather_cuts[1:]))
+    back_parts = list(zip(back_cuts[:-1], back_cuts[1:]))
     section = lax.axis_index("section")
     me = lax.axis_index("dp")
     core = lax.rem(me, 2)
@@ -222,7 +225,7 @@
         right = jnp.broadcast_to(gains[:, columns(q, 1)], (seg_rows, own_cols))
         gains_p[:, part(q)] = jnp.where(low_rows(left.shape), left, right)
     for m in range(micro):
-        slot = jnp.clip(ids[m, 0] - me * slot_count, 0, slot_count - 1)
+        slot = jnp.clip(ids[m] - me * slot_count, 0, slot_count - 1)
         pack(acts[m].astype(F32), acts_p, 2 * m)
         pack(stored[0, slot].astype(F32), before_p, 2 * m)
         pack(cotangent[m].astype(F32), cotangent_p, 2 * m)
@@ -282,11 +285,10 @@
 
     def turn_normed(m):
         for q in range(quarter):
-            p, start = (q * own_cols) // span, (q * own_cols) % span
             sides = [[], []]
             for chain in range(2):
                 one, two = (
-                    gbuf[2 * m + u, chain, p, :, :, start : start + own_cols].astype(F32)
+                    gbuf[2 * m + u, chain, :, :, part(q)].astype(F32)
                     for u in range(2)
                 )
                 for h, whole in enumerate(unpack(one, two)):
@@ -304,29 +306,43 @@
             copy_sem.at[m, chain],
         )
 
-    def send_slopes(kind, e, there, remote_own):
+    def send_shares(e):
         def send(step, carry):
             other = far_device(step)
             remote(
-                slopes.at[kind, e, lax.div(other, 2)],
+                slopes.at[1, e, lax.div(other, 2)],
                 slope_in.at[e, core, chip],
-                slope_send.at[kind, e],
+                slope_send.at[1, e],
                 slope_recv.at[e, core],
-                there,
+                section,
                 other,
             ).start()
             return carry
 
-        if remote_own:
-            lax.fori_loop(0, groups, send, 0)
-        else:
-            lax.fori_loop(0, groups - 1, send, 0)
-            pltpu.make_async_copy(
-                slopes.at[kind, e, chip], slope_in.at[e, core, chip], slope_recv.at[e, core]
-            ).start()
-
-    def summed_parts(kind, e, q):
-        return pin[kind, e, 2 * q].astype(F32) + pin[kind, e, 2 * q + 1].astype(F32)
+        lax.fori_loop(0, groups - 1, send, 0)
+        pltpu.make_async_copy(
+            slopes.at[1, e, chip], slope_in.at[e, core, chip], slope_recv.at[e, core]
+        ).start()
+
+    @pl.when(last)
+    def _():
+        def share(e, carry):
+            for q in range(chips):
+                slopes[1, e, q] = cotangent_p[e, :, part(q)]
+            send_shares(e)
+            return carry
+
+        lax.fori_loop(0, sets, share, 0)
+
+    def pair_copy(e, chain):
+        return remote(
+            pout.at[e, chain],
+            pair_in.at[e, chain],
+            part_send.at[e, chain],
+            pair_recv.at[e, chain],
+            section,
+            sibling,
+        )
 
     def forward_rows(e):
         @pl.when(first & (e == 0) & (core == 1))
@@ -340,9 +356,9 @@
         @pl.when(jnp.logical_not(first))
         def _():
             await_bytes(arr_in.at[e], side_recv.at[0, e])
-            await_bytes(pin.at[0, e], part_recv.at[0, e])
+            await_bytes(pin.at[e], part_recv.at[e])
             for q in range(chips):
-                value = summed_parts(0, e, q)
+                value = pin[e, 2 * q].astype(F32) + pin[e, 2 * q + 1].astype(F32)
                 hidden[e, :, part(q)] = value
                 total = arr_in[e, :, part(q)].astype(F32) + gelu_value(value)
                 incoming[:, part(q)] = total.astype(BF16).astype(F32)
@@ -356,16 +372,15 @@
         scales[e] = jnp.broadcast_to(scale, (seg_rows, 128))
         normed = (arrived_f * scale * gains_p[...]).astype(BF16)
         for side in range(2):
-            for p in range(parts):
-                start = side * fold + p * span
-                nbuf[e, p, side] = normed[:, start : start + span]
-        for p in range(parts):
-
-            def send(step, carry, p=p):
+            nbuf[e, side] = normed[:, side * fold : (side + 1) * fold]
+        for p, (low_end, high_end) in enumerate(gather_parts):
+            cut = slice(low_end, high_end)
+
+            def send(step, carry, p=p, cut=cut):
                 other = far_device(step)
                 remote(
-                    nbuf.at[e, p, lax.rem(other, 2)],
-                    gbuf.at[e, core, p, chip],
+                    nbuf.at[e, lax.rem(other, 2), :, cut],
+                    gbuf.at[e, core, chip, :, cut],
                     gather_send.at[e],
                     gather_recv.at[e, core, p],
                     section,
@@ -373,9 +388,11 @@
                 ).start()
                 return carry
 
-            lax.fori_loop(0, groups - 1, send, 0)
+            lax.fori_loop(0, groups - 1, send, 0, unroll=True)
             pltpu.make_async_copy(
-                nbuf.at[e, p, core], gbuf.at[e, core, p, chip], gather_recv.at[e, core, p]
+                nbuf.at[e, core, :, cut],
+                gbuf.at[e, core, chip, :, cut],
+                gather_recv.at[e, core, p],
             ).start()
 
         @pl.when(jnp.logical_not(last))
@@ -395,8 +412,8 @@
             await_bytes(wbuf.at[:, :, own_place], w_sem.at[2])
             await_bytes(wbuf.at[:, :, own_place], w_sem.at[1])
 
-        for p in range(parts):
-            await_bytes(gbuf.at[e, chain, p], gather_recv.at[e, chain, p])
+        for p, (base, high_end) in enumerate(gather_parts):
+            await_bytes(gbuf.at[e, chain, :, :, base:high_end], gather_recv.at[e, chain, p])
             if p == 0:
 
                 @pl.when(first & (e == 0) & (chain == 0) & (core == 0))
@@ -405,14 +422,13 @@
                         stagger, inc=1, device_id={"dp": sibling}, device_id_type=MESH
                     )
 
-            base = p * span
-            piece = gbuf[e, chain, p].astype(F32).reshape(rows, span)
-            xbuf[:, base : base + span] = piece.astype(BF16)
+            piece = gbuf[e, chain, :, :, base:high_end].astype(F32)
+            xbuf[:, base:high_end] = piece.reshape(rows, high_end - base).astype(BF16)
             for h in range(2):
                 for c in range(0, chip_cols, 256):
                     product = jnp.dot(
-                        xbuf[:, base : base + span],
-                        wbuf[h, base : base + span, c : c + 256],
+                        xbuf[:, base:high_end],
+                        wbuf[h, base:high_end, c : c + 256],
                         preferred_element_type=F32,
                     )
                     if p > 0:
@@ -432,51 +448,37 @@
             q = far_chip(step)
             other = 2 * q + chain
 
-            @pl.when(jnp.logical_not(last))
-            def _():
-                remote(
-                    pout.at[e, chain, q],
-                    pin.at[0, e, me],
-                    part_send.at[e, chain],
-                    part_recv.at[0, e],
-                    after,
-                    other,
-                ).start()
-
-            @pl.when(last & (other != me))
-            def _():
-                remote(
-                    pout.at[e, chain, q],
-                    pin.at[1, e, me],
-                    part_send.at[e, chain],
-                    part_recv.at[1, e],
-                    section,
-                    other,
-                ).start()
-
+            remote(
+                pout.at[e, chain, q],
+                pin.at[e, me],
+                part_send.at[e, chain],
+                part_recv.at[e],
+                after,
+                other,
+            ).start()
             return carry
 
-        lax.fori_loop(0, chips, send, 0)
-
-        @pl.when(last & (core == chain))
-        def _():
-            pltpu.make_async_copy(
-                pout.at[e, chain, chip], pin.at[1, e, me], part_recv.at[1, e]
-            ).start()
-
-    def turn_rows(e):
-        await_bytes(pin.at[1, e], part_recv.at[1, e])
-        for q in range(chips):
-            slope = cotangent_p[e, :, part(q)].astype(F32) * gelu_slope(summed_parts(1, e, q))
-            slopes[1, e, q] = slope.astype(BF16)
-        send_slopes(1, e, section, False)
+        @pl.when(jnp.logical_not(last))
+        def _():
+            lax.fori_loop(0, chips, send, 0, unroll=True)
+
+        @pl.when(last)
+        def _():
+            pair_copy(e, chain).start()
 
     def backward_columns(e, chain):
         await_bytes(slope_in.at[e, chain], slope_recv.at[e, chain])
+
+        @pl.when(last)
+        def _():
+            pair_copy(e, chain).wait_recv()
+            value = pout[e, chain].astype(F32) + pair_in[e, chain].astype(F32)
+            slope = slope_in[e, chain].astype(F32) * gelu_slope(value)
+            slope_in[e, chain] = slope.astype(BF16)
+
         ybuf[...] = slope_in[e, chain].astype(F32).reshape(rows, own_cols).astype(BF16)
-        for p in range(parts):
-            for k in range(0, span, step_b):
-                start = p * span + k
+        for p, (low_end, high_end) in enumerate(back_parts):
+            for start in range(low_end, high_end, step_b):
                 shape = (chips, seg_rows, step_b)
                 terms = [
                     [
@@ -492,21 +494,23 @@
                 ]
                 left = terms[0][0] + turned(terms[0][1])
                 right = turned(terms[1][0]) + terms[1][1]
-                back_out[e, chain, p, :, :, k : k + step_b] = jnp.where(
+                back_out[e, chain, :, :, start : start + step_b] = jnp.where(
                     low_rows(shape), left, right
                 ).astype(BF16)
 
-            def send(step, carry, p=p):
+            cut = slice(low_end, high_end)
+
+            def send(step, carry, p=p, cut=cut):
                 q = far_chip(step)
                 other = 2 * q + chain
 
                 @pl.when(other != me)
                 def _():
                     remote(
-                        back_out.at[e, chain, p, q],
-                        back_in.at[e, p, me],
+                        back_out.at[e, chain, q, :, cut],
+                        back_in.at[e, me, :, cut],
                         back_send.at[e, chain],
-                        back_recv.at[e],
+                        back_recv.at[e, p],
                         section,
                         other,
                     ).start()
@@ -515,17 +519,20 @@
 
             @pl.when(jnp.logical_not(first))
             def _(p=p, send=send):
-                lax.fori_loop(0, chips, send, 0)
+                lax.fori_loop(0, chips, send, 0, unroll=True)
 
             @pl.when(jnp.logical_not(first) & (core == chain))
-            def _(p=p):
+            def _(p=p, cut=cut):
                 pltpu.make_async_copy(
-                    back_out.at[e, chain, p, chip], back_in.at[e, p, me], back_recv.at[e]
+                    back_out.at[e, chain, chip, :, cut],
+                    back_in.at[e, me, :, cut],
+                    back_recv.at[e, p],
                 ).start()
 
-        for p in range(parts):
-            term = back_out[e, chain, p].astype(F32) * gbuf[e, chain, p].astype(F32)
-            gain_sum[:, p * span : (p + 1) * span] += jnp.sum(term, axis=0)
+        for start in range(0, fold, 512):
+            cut = slice(start, start + 512)
+            term = back_out[e, chain, :, :, cut].astype(F32) * gbuf[e, chain, :, :, cut].astype(F32)
+            gain_sum[:, cut] += jnp.sum(term, axis=0)
 
         @pl.when(lax.rem(e, 2) == 1)
         def _():
@@ -546,25 +553,39 @@
         def _():
             await_bytes(up_in.at[e], side_recv.at[1, e])
 
-        await_bytes(back_in.at[e], back_recv.at[e])
-        pieces = []
-        for side in range(2):
-            for p in range(parts):
-                total = back_in[e, p, side].astype(F32)
+        for p, (low_end, high_end) in enumerate(back_parts):
+            cut = slice(low_end, high_end)
+            await_bytes(back_in.at[e, :, :, cut], back_recv.at[e, p])
+            for side in range(2):
+                total = back_in[e, side, :, cut].astype(F32)
                 for q in range(1, chips):
-                    total = total + back_in[e, p, 2 * q + side].astype(F32)
-                pieces.append(total)
-        back = jnp.concatenate(pieces, axis=1)
+                    total = total + back_in[e, 2 * q + side, :, cut].astype(F32)
+                incoming[:, side * fold + low_end : side * fold + high_end] = total
+        back = incoming[...]
         arrived_f = arrived[e].astype(F32)
         scale = scales[e][:, :1]
         weighted = back * gains_p[...]
         mean_term = row_mean(weighted * arrived_f)
         total = up_in[e].astype(F32) + scale * (weighted - arrived_f * scale * scale * mean_term)
         up_out[e] = total.astype(BF16)
-        for q in range(chips):
-            slope = up_out[e, :, part(q)].astype(F32) * hidden[e, :, part(q)]
+
+        def send(step, carry):
+            q = far_chip(step)
+            place = pl.ds(pl.multiple_of(q * own_cols, 128), own_cols)
+            slope = up_out[e, :, place].astype(F32) * hidden[e, :, place]
             slopes[0, e, q] = slope.astype(BF16)
-        send_slopes(0, e, before, True)
+            for c in range(2):
+                remote(
+                    slopes.at[0, e, q],
+                    slope_in.at[e, core, chip],
+                    slope_send.at[0, e],
+                    slope_recv.at[e, core],
+                    before,
+                    2 * q + c,
+                ).start()
+            return carry
+
+        lax.fori_loop(0, chips, send, 0, unroll=True)
 
         @pl.when(section > 1)
         def _():
@@ -572,7 +593,7 @@
                 up_out.at[e], up_in.at[e], side_send.at[1, e], side_recv.at[1, e], before, me
             ).start()
 
-    FR, FC, TR, BC, BR, TN, NO = range(7)
+    FR, FC, BC, BR, TN, NO = range(6)
     orders = [[make_order(micro, where, side) for side in range(2)] for where in range(2)]
     length = max(len(order) for pair in orders for order in pair)
     for pair in orders:
@@ -593,7 +614,6 @@
         chain = lax.rem(now, 2)
         pl.when(kind == FR)(lambda: forward_rows(e))
         pl.when(kind == FC)(lambda: forward_columns(e, chain))
-        pl.when(kind == TR)(lambda: turn_rows(e))
         pl.when(kind == BC)(lambda: backward_columns(e, chain))
         pl.when((kind == BR) & jnp.logical_not(first))(lambda: backward_rows(e))
         pl.when(kind == TN)(lambda: turn_normed(lax.div(e, 2)))
@@ -631,21 +651,13 @@
     arrived_copy.start()
     await_bytes(wbuf.at[:, :, own_place], w_sem.at[0])
     for e in range(sets):
-        for p in range(parts):
-            await_bytes(back_in.at[e, p, 0 : groups - 1], gather_send.at[e])
+        await_bytes(back_in.at[e, 0 : groups - 1], gather_send.at[e])
         for chain in range(2):
-
-            @pl.when(last & (core == chain))
-            def _(e=e, chain=chain):
-                await_bytes(pout.at[e, chain, 0 : chips - 1], part_send.at[e, chain])
-
-            @pl.when(jnp.logical_not(last & (core == chain)))
-            def _(e=e, chain=chain):
-                await_bytes(pout.at[e, chain], part_send.at[e, chain])
+            await_bytes(pout.at[e, chain], part_send.at[e, chain])
 
             @pl.when(jnp.logical_not(first) & (core == chain))
             def _(e=e, chain=chain):
-                await_bytes(back_out.at[e, chain, :, 0 : chips - 1], back_send.at[e, chain])
+                await_bytes(back_out.at[e, chain, 0 : chips - 1], back_send.at[e, chain])
 
             @pl.when(jnp.logical_not(first) & (core != chain))
             def _(e=e, chain=chain):
@@ -653,11 +665,11 @@
 
         @pl.when(last)
         def _(e=e):
-            await_bytes(pin.at[1, e, 0 : groups - 1], slope_send.at[1, e])
+            await_bytes(pin.at[e, 0 : groups - 1], slope_send.at[1, e])
 
         @pl.when(jnp.logical_not(first))
         def _(e=e):
-            await_bytes(pin.at[0, e], slope_send.at[0, e])
+            await_bytes(pin.at[e], slope_send.at[0, e])
 
         @pl.when(section > 1)
         def _(e=e):
@@ -695,8 +707,7 @@
     chips = groups // 2
     rows = chips * seg_rows
     sets = 2 * micro
-    parts = part_count
-    span = fold // parts
+    flat_ids = sample_ids.reshape(micro)
     anywhere = pl.BlockSpec(memory_space=pl.ANY)
     smem = pl.BlockSpec(memory_space=pltpu.SMEM)
     dma = pltpu.SemaphoreType.DMA
@@ -720,12 +731,13 @@
             pltpu.VMEM((sets, seg_rows, half), BF16),
             pltpu.VMEM((seg_rows, half), F32),
             pltpu.VMEM((2, fold, chip_cols), BF16),
-            pltpu.VMEM((sets, parts, 2, seg_rows, span), BF16),
-            pltpu.VMEM((sets, 2, parts, chips, seg_rows, span), BF16),
+            pltpu.VMEM((sets, 2, seg_rows, fold), BF16),
+            pltpu.VMEM((sets, 2, chips, seg_rows, fold), BF16),
             pltpu.VMEM((rows, fold), BF16),
             pltpu.VMEM((2, rows, chip_cols), F32),
             pltpu.VMEM((sets, 2, chips, seg_rows, own_cols), BF16),
-            pltpu.VMEM((2, sets, groups, seg_rows, own_cols), BF16),
+            pltpu.VMEM((sets, groups, seg_rows, own_cols), BF16),
+            pltpu.VMEM((sets, 2, chips, seg_rows, own_cols), BF16),
             pltpu.VMEM((sets, seg_rows, half), F32),
             pltpu.VMEM((seg_rows, half), F32),
             pltpu.VMEM((sets, seg_rows, half), BF16),
@@ -735,8 +747,8 @@
             pltpu.VMEM((sets, 2, chips, seg_rows, own_cols), BF16),
             pltpu.VMEM((rows, own_cols), BF16),
             pltpu.VMEM((micro, 2, rows, own_cols), BF16),
-            pltpu.VMEM((sets, 2, parts, chips, seg_rows, span), BF16),
-            pltpu.VMEM((sets, parts, groups, seg_rows, span), BF16),
+            pltpu.VMEM((sets, 2, chips, seg_rows, fold), BF16),
+            pltpu.VMEM((sets, groups, seg_rows, fold), BF16),
             pltpu.VMEM((sets, seg_rows, half), BF16),
             pltpu.VMEM((sets, seg_rows, half), BF16),
             pltpu.VMEM((sets, seg_rows, 128), F32),
@@ -748,13 +760,14 @@
             dma((4,)),
             dma((3,)),
             dma((sets,)),
-            dma((sets, 2, parts)),
+            dma((sets, 2, len(gather_cuts) - 1)),
             dma((sets, 2)),
-            dma((2, sets)),
+            dma((sets,)),
+            dma((sets, 2)),
             dma((2, sets)),
             dma((sets, 2)),
             dma((sets, 2)),
-            dma((sets,)),
+            dma((sets, len(back_cuts) - 1)),
             dma((2, sets)),
             dma((2, sets)),
             dma((micro,)),
@@ -767,9 +780,9 @@
         compiler_params=pltpu.CompilerParams(
             collective_id=0, has_side_effects=True, vmem_limit_bytes=60 * 1024 * 1024
         ),
-    )(sample_ids, acts_in, weights, gains, stored, cotangent)
-
-    block_k = 512
+    )(flat_ids, acts_in, weights, gains, stored, cotangent)
+
+    block_k = 1536
     blocks = width // block_k
     slot_count = stored.shape[1]
 
@@ -808,7 +821,7 @@
         side[1].wait()
         side[2].wait()
         for m in range(micro):
-            slot = ids_ref[m, 0] - lax.axis_index("dp") * slot_count
+            slot = ids_ref[m] - lax.axis_index("dp") * slot_count
             kept_buf[0, jnp.clip(slot, 0, slot_count - 1)] = arrived_buf[m]
         kept_copy = pltpu.make_async_copy(kept_buf, kept_ref, side_sem.at[4])
         kept_copy.start()
@@ -837,7 +850,7 @@
             dma((5,)),
         ],
         compiler_params=pltpu.CompilerParams(vmem_limit_bytes=60 * 1024 * 1024),
-    )(sample_ids, normed, slope, stored, arrived, gain)
+    )(flat_ids, normed, slope, stored, arrived, gain)
     return (kept, grad, gain)
 
 

time: 241 us -> 223 us (0.925)
  Pallas kernels: 239 us -> 222 us
    pallas_call x1, Pallas kernels: 232 us -> 216 us  [on_device(): pl.pallas_call(functools.partial(relay, sections, groups), out_shape=(jax...]
where the time goes in v2:
time: 223 us
  Pallas kernels  222 us (100%)
    pallas_call x1, Pallas kernels, on_device(): pl.pallas_call(functools.partial(relay, sections, groups), out_shape=(jax...  216 us
    pallas_call x1, Pallas kernels, on_device(): pl.pallas_call(finish, out_shape=(jax.ShapeDtypeStruct(stored.shape, BF16...  6.24 us

profile of v2, /device:TPU:1, one launch (start us, length us, event | category | flops | bytes accessed | tf_op | source)
XLA Modules:
  0.0 222.6 jit_solution(8719574101576405587)
XLA Ops:
  0.6 215.7 %shard_map.85 = (bf16[2,8,6144]{2,1,0:T(8,128)(2,1)}, bf16[6144,256]{1,0:T(8,128)(2,1)}, bf16[256,384]{1,0:T(8,128)(2,1)}, f32[1,6144]{1,0:T(1,128)}) custom-call(s32[2]{0:T(128)} %bitcast.1, bf16[2,8,6144]{2,1,0:T(8,128)(2,1)} %acts_hbm.1, bf16[1,6144,384]{2,1,0:T(8,128)(2,1)} %weights.1, f32[1,6144]{1,0:T(1,128)} %gains_hbm.1, ...), custom_call_target="tpu_custom_call" | custom-call | tf_op jit(solution)/shard_map/pallas_call | solution.py:714
  216.3 6.2 %shard_map.86 = (bf16[1,4,8,6144]{3,2,1,0:T(8,128)(2,1)}, f32[1,6144,384]{2,1,0:T(8,128)}, f32[1,6144]{1,0:T(1,128)}) custom-call(s32[2]{0:T(128)} %bitcast.2, bf16[6144,256]{1,0:T(8,128)(2,1)} %get-tuple-element.7.normed_ref, bf16[256,384]{1,0:T(8,128)(2,1)} %get-tuple-element.8.slope_ref, bf16[1,4,8,6144]{3,2,1,0:T(8,128)(2,1)} %stored_ref.1, ...), custom_call_target="tpu_custom_call" | custom-call | tf_op jit(solution)/shard_map/pallas_call | solution.py:833

commit v3 on v2

--- a/solution.py
+++ b/solution.py
@@ -145,6 +145,25 @@
     z_pos = lax.div(me, 4)
     x_pos = lax.rem(chip, 2)
 
+    barrier = pltpu.get_barrier_semaphore()
+
+    def greet(step, carry):
+        other = lax.rem(me + step, groups)
+        for there in (after, before):
+            pl.semaphore_signal(
+                barrier, inc=1, device_id={"section": there, "dp": other}, device_id_type=MESH
+            )
+
+        @pl.when(step > 0)
+        def _():
+            pl.semaphore_signal(
+                barrier, inc=1, device_id={"section": section, "dp": other}, device_id_type=MESH
+            )
+
+        return carry
+
+    lax.fori_loop(0, groups, greet, 0, unroll=True)
+
     loads = [
         pltpu.make_async_copy(source, target, load_sem.at[i])
         for i, (source, target) in enumerate(
@@ -173,25 +192,6 @@
     for source, target in weight_pieces(core):
         pltpu.make_async_copy(source, target, w_sem.at[2]).start()
 
-    barrier = pltpu.get_barrier_semaphore()
-
-    def greet(step, carry):
-        other = lax.rem(me + step, groups)
-        for there in (after, before):
-            pl.semaphore_signal(
-                barrier, inc=1, device_id={"section": there, "dp": other}, device_id_type=MESH
-            )
-
-        @pl.when(step > 0)
-        def _():
-            pl.semaphore_signal(
-                barrier, inc=1, device_id={"section": section, "dp": other}, device_id_type=MESH
-            )
-
-        return carry
-
-    lax.fori_loop(0, groups, greet, 0)
-
     def part(q):
         return slice(q * own_cols, (q + 1) * own_cols)
 
@@ -217,6 +217,10 @@
     def unpack(one, two):
         low = low_rows(one.shape)
         return jnp.where(low, one, turned(two)), jnp.where(low, turned(one), two)
+
+    def double(packed):
+        low, other = low_rows(packed.shape), turned(packed)
+        return jnp.where(low, packed, other), jnp.where(low, other, packed)
 
     for load in loads:
         load.wait()
@@ -423,26 +427,26 @@
                     )
 
             piece = gbuf[e, chain, :, :, base:high_end].astype(F32)
-            xbuf[:, base:high_end] = piece.reshape(rows, high_end - base).astype(BF16)
-            for h in range(2):
-                for c in range(0, chip_cols, 256):
-                    product = jnp.dot(
-                        xbuf[:, base:high_end],
+            for h, whole in enumerate(double(piece)):
+                xbuf[h, :, base:high_end] = whole.reshape(rows, high_end - base).astype(BF16)
+            for c in range(0, chip_cols, 256):
+                product = sum(
+                    jnp.dot(
+                        xbuf[h, :, base:high_end],
                         wbuf[h, base:high_end, c : c + 256],
                         preferred_element_type=F32,
                     )
-                    if p > 0:
-                        product = product + products[h, :, c : c + 256]
-                    products[h, :, c : c + 256] = product
+                    for h in range(2)
+                )
+                if p > 0:
+                    product = product + products[:, c : c + 256]
+                products[:, c : c + 256] = product
         shape = (chips, seg_rows, own_cols)
-        left = products[0, :, :own_cols].reshape(shape) + turned(
-            products[1, :, :own_cols].reshape(shape)
-        )
-        right = (
-            turned(products[0, :, own_cols:].reshape(shape))
-            + products[1, :, own_cols:].reshape(shape)
-        )
-        pout[e, chain] = jnp.where(low_rows(shape), left, right).astype(BF16)
+        pout[e, chain] = jnp.where(
+            low_rows(shape),
+            products[:, :own_cols].reshape(shape),
+            products[:, own_cols:].reshape(shape),
+        ).astype(BF16)
 
         def send(step, carry):
             q = far_chip(step)
@@ -476,24 +480,20 @@
             slope = slope_in[e, chain].astype(F32) * gelu_slope(value)
             slope_in[e, chain] = slope.astype(BF16)
 
-        ybuf[...] = slope_in[e, chain].astype(F32).reshape(rows, own_cols).astype(BF16)
+        for s, whole in enumerate(double(slope_in[e, chain].astype(F32))):
+            ybuf[:, part(s)] = whole.reshape(rows, own_cols).astype(BF16)
         for p, (low_end, high_end) in enumerate(back_parts):
             for start in range(low_end, high_end, step_b):
                 shape = (chips, seg_rows, step_b)
-                terms = [
-                    [
-                        lax.dot_general(
-                            ybuf[...],
-                            wbuf[h, start : start + step_b, s * own_cols : (s + 1) * own_cols],
-                            (((1,), (1,)), ((), ())),
-                            preferred_element_type=F32,
-                        ).reshape(shape)
-                        for s in range(2)
-                    ]
+                left, right = (
+                    lax.dot_general(
+                        ybuf[...],
+                        wbuf[h, start : start + step_b, :],
+                        (((1,), (1,)), ((), ())),
+                        preferred_element_type=F32,
+                    ).reshape(shape)
                     for h in range(2)
-                ]
-                left = terms[0][0] + turned(terms[0][1])
-                right = turned(terms[1][0]) + terms[1][1]
+                )
                 back_out[e, chain, :, :, start : start + step_b] = jnp.where(
                     low_rows(shape), left, right
                 ).astype(BF16)
@@ -637,7 +637,7 @@
         ).start()
         return carry
 
-    lax.fori_loop(0, groups - 1, gain_send, 0)
+    lax.fori_loop(0, groups - 1, gain_send, 0, unroll=True)
     pltpu.make_async_copy(gain_row, gain_in.at[me], gain_sem.at[1]).start()
 
     for m in range(micro):
@@ -733,8 +733,8 @@
             pltpu.VMEM((2, fold, chip_cols), BF16),
             pltpu.VMEM((sets, 2, seg_rows, fold), BF16),
             pltpu.VMEM((sets, 2, chips, seg_rows, fold), BF16),
-            pltpu.VMEM((rows, fold), BF16),
-            pltpu.VMEM((2, rows, chip_cols), F32),
+            pltpu.VMEM((2, rows, fold), BF16),
+            pltpu.VMEM((rows, chip_cols), F32),
             pltpu.VMEM((sets, 2, chips, seg_rows, own_cols), BF16),
             pltpu.VMEM((sets, groups, seg_rows, own_cols), BF16),
             pltpu.VMEM((sets, 2, chips, seg_rows, own_cols), BF16),
@@ -745,7 +745,7 @@
             pltpu.VMEM((sets, seg_rows, half), BF16),
             pltpu.VMEM((2, sets, chips, seg_rows, own_cols), BF16),
             pltpu.VMEM((sets, 2, chips, seg_rows, own_cols), BF16),
-            pltpu.VMEM((rows, own_cols), BF16),
+            pltpu.VMEM((rows, chip_cols), BF16),
             pltpu.VMEM((micro, 2, rows, own_cols), BF16),
             pltpu.VMEM((sets, 2, chips, seg_rows, fold), BF16),
             pltpu.VMEM((sets, groups, seg_rows, fold), BF16),

time: 223 us -> 223 us (level)
  no operation moved by 1% of the time
where the time goes in v3:
time: 223 us; the launch traced here: 222 us
  Pallas kernels  222 us (100%)
    pallas_call x1, Pallas kernels, on_device(): pl.pallas_call(functools.partial(relay, sections, groups), out_shape=(jax...  216 us
    pallas_call x1, Pallas kernels, on_device(): pl.pallas_call(finish, out_shape=(jax.ShapeDtypeStruct(stored.shape, BF16...  6.24 us

profile of v3, /device:TPU:1, one launch (start us, length us, event | category | flops | bytes accessed | tf_op | source)
XLA Modules:
  0.0 222.5 jit_solution(13736506271828028334)
XLA Ops:
  0.6 215.6 %shard_map.85 = (bf16[2,8,6144]{2,1,0:T(8,128)(2,1)}, bf16[6144,256]{1,0:T(8,128)(2,1)}, bf16[256,384]{1,0:T(8,128)(2,1)}, f32[1,6144]{1,0:T(1,128)}) custom-call(s32[2]{0:T(128)} %bitcast.1, bf16[2,8,6144]{2,1,0:T(8,128)(2,1)} %acts_hbm.1, bf16[1,6144,384]{2,1,0:T(8,128)(2,1)} %weights.1, f32[1,6144]{1,0:T(1,128)} %gains_hbm.1, ...), custom_call_target="tpu_custom_call" | custom-call | tf_op jit(solution)/shard_map/pallas_call | solution.py:714
  216.3 6.2 %shard_map.86 = (bf16[1,4,8,6144]{3,2,1,0:T(8,128)(2,1)}, f32[1,6144,384]{2,1,0:T(8,128)}, f32[1,6144]{1,0:T(1,128)}) custom-call(s32[2]{0:T(128)} %bitcast.2, bf16[6144,256]{1,0:T(8,128)(2,1)} %get-tuple-element.7.normed_ref, bf16[256,384]{1,0:T(8,128)(2,1)} %get-tuple-element.8.slope_ref, bf16[1,4,8,6144]{3,2,1,0:T(8,128)(2,1)} %stored_ref.1, ...), custom_call_target="tpu_custom_call" | custom-call | tf_op jit(solution)/shard_map/pallas_call | solution.py:833

commit v4 on v2

--- a/solution.py
+++ b/solution.py
@@ -28,6 +28,7 @@
     )
 
 
+device_steps = ((2, 1, 1), (2, 1, 0), (1, 1, 1), (1, 1, 0), (3, 1, 1), (3, 1, 0), (2, 0, 1), (2, 0, 0), (0, 1, 1), (0, 1, 0), (1, 0, 1), (1, 0, 0), (3, 0, 1), (3, 0, 0), (0, 0, 1))
 gather_cuts = (0, 768, 1280, 1536)
 back_cuts = (0, 512, 1024, 1536)
 step_b = 256
@@ -250,6 +251,13 @@
         return lax.rem(z_pos + away, z_count)
 
     def far_device(i):
+        if isinstance(i, int):
+            z, x, c = device_steps[i]
+            return (
+                lax.rem(z_pos + z, z_count) * 4
+                + lax.rem(x_pos + x, 2) * 2
+                + lax.rem(core + c, 2)
+            )
         x = lax.rem(x_pos + 1 - lax.rem(lax.div(i, 2), 2), 2)
         return far_z(lax.div(i, 4)) * 4 + x * 2 + lax.rem(core + 1 - lax.rem(i, 2), 2)
 
@@ -388,7 +396,8 @@
                 ).start()
                 return carry
 
-            lax.fori_loop(0, groups - 1, send, 0, unroll=True)
+            for step in range(groups - 1):
+                send(step, 0)
             pltpu.make_async_copy(
                 nbuf.at[e, core, :, cut],
                 gbuf.at[e, core, chip, :, cut],

time: 223 us -> 223 us (level)
  no operation moved by 1% of the time
where the time goes in v4:
time: 223 us
  Pallas kernels  222 us (100%)
    pallas_call x1, Pallas kernels, on_device(): pl.pallas_call(functools.partial(relay, sections, groups), out_shape=(jax...  216 us
    pallas_call x1, Pallas kernels, on_device(): pl.pallas_call(finish, out_shape=(jax.ShapeDtypeStruct(stored.shape, BF16...  6.24 us

profile of v4, /device:TPU:1, one launch (start us, length us, event | category | flops | bytes accessed | tf_op | source)
XLA Modules:
  0.0 222.7 jit_solution(15106220253704022873)
XLA Ops:
  0.6 215.8 %shard_map.85 = (bf16[2,8,6144]{2,1,0:T(8,128)(2,1)}, bf16[6144,256]{1,0:T(8,128)(2,1)}, bf16[256,384]{1,0:T(8,128)(2,1)}, f32[1,6144]{1,0:T(1,128)}) custom-call(s32[2]{0:T(128)} %bitcast.1, bf16[2,8,6144]{2,1,0:T(8,128)(2,1)} %acts_hbm.1, bf16[1,6144,384]{2,1,0:T(8,128)(2,1)} %weights.1, f32[1,6144]{1,0:T(1,128)} %gains_hbm.1, ...), custom_call_target="tpu_custom_call" | custom-call | tf_op jit(solution)/shard_map/pallas_call | solution.py:723
  216.4 6.2 %shard_map.86 = (bf16[1,4,8,6144]{3,2,1,0:T(8,128)(2,1)}, f32[1,6144,384]{2,1,0:T(8,128)}, f32[1,6144]{1,0:T(1,128)}) custom-call(s32[2]{0:T(128)} %bitcast.2, bf16[6144,256]{1,0:T(8,128)(2,1)} %get-tuple-element.7.normed_ref, bf16[256,384]{1,0:T(8,128)(2,1)} %get-tuple-element.8.slope_ref, bf16[1,4,8,6144]{3,2,1,0:T(8,128)(2,1)} %stored_ref.1, ...), custom_call_target="tpu_custom_call" | custom-call | tf_op jit(solution)/shard_map/pallas_call | solution.py:842
